TPU v7x, 512 devices: a whole 4x8x8 slice. The times are simulated.
512 devices in a mesh: mp: 32 (over z, y_lo), dp: 16 (over x, y_hi, core).
Axes of the slice: x: 4, y: 8 (y_hi: 2, y_lo: 4; y = y_hi * 4 + y_lo), z: 8, core: 2. Of those that a mesh axis runs over, the one named last changes fastest.
Arguments:
- forward_fields: bfloat16 [16, 4, 65536], P(None, None, 'mp'), may hold values from -6 to 6
- adjoint_fields: bfloat16 [64, 4, 65536], P(None, None, 'mp'), may hold values from -6 to 6
- data_rec: int32 [3072], P('dp'), may hold values from 0 to 63
- data_freq: int32 [3072], P('dp'), may hold values from 0 to 15
- data_coef: float32 [3072, 4], P('dp'), may hold values from -6 to 6
- residual_cols: bfloat16 [3072, 256], P('dp'), may hold values from -6 to 6
Outputs:
- data_update: bfloat16 [3072, 256], P('dp')
- model_update: float32 [65536, 256], P(('mp', 'dp'))
All inputs are finite; a program needn't handle non-finite values.
Results may differ from a plain program's by a relative error of at most 0.0075.
Values may be sent and summed in bfloat16 or wider, within the bound.
No kernel may reach another device: no remote copies, remote signals or barrier semaphores. Data moves between devices by JAX's collectives and lax.ppermute only.
A program may use at most 64 MiB of HBM per device.

v0:
```python
import math
import jax
import jax.numpy as jnp
from jax import lax
from jax.sharding import PartitionSpec as P

GRID_COLS = 128
SWEEPS = 2


def with_halo(array, sides, width):
    for axis, dim in sides:
        peers, length = (lax.axis_size(axis), array.shape[dim])
        up = [(i, (i + 1) % peers) for i in range(peers - 1)]
        down = [(j, i) for i, j in up]
        last = lax.slice_in_dim(array, length - width, length, axis=dim)
        leading = lax.slice_in_dim(array, 0, width, axis=dim)
        before = lax.ppermute(last, axis, up)
        after = lax.ppermute(leading, axis, down)
        array = jnp.concatenate([before, array, after], axis=dim)
    return array


def sweep_once(field):
    center = field[:, 1:-1, :]
    sides = jnp.pad(center, ((0, 0), (0, 0), (1, 1)))
    beside_all = field[:, :-2, :] + field[:, 2:, :] + sides[:, :, :-2] + sides[:, :, 2:]
    return center + 0.2 * (beside_all - 4.0 * center)


def per_device(forward_fields, adjoint_fields, data_rec, data_freq, data_coef, residual_cols):
    rows_here = data_rec.shape[0]
    cells_here = forward_fields.shape[2]
    slab_rows = cells_here // GRID_COLS
    slab_count = lax.axis_size("mp")
    block_count = lax.axis_size("dp")
    adjoint = adjoint_fields[data_rec].astype(jnp.float32)
    forward = forward_fields[data_freq].astype(jnp.float32)
    sens = (0.5 * jnp.sum(data_coef[:, :, None] * adjoint * forward, axis=1)).astype(jnp.bfloat16)
    grid = sens.astype(jnp.float32).reshape(rows_here, slab_rows, GRID_COLS)
    for sweep in range(SWEEPS):
        padded = with_halo(grid, (("mp", 1),), 1)
        grid = sweep_once(padded)
    smooth = grid.reshape(rows_here, cells_here).astype(jnp.bfloat16)
    residual_whole = lax.all_gather(residual_cols, "dp", axis=0, tiled=True)
    gram_tile = lax.dot_general(
        smooth,
        lax.all_gather(sens, "dp", axis=0, tiled=True),
        (((1,), (1,)), ((), ())),
        preferred_element_type=jnp.float32,
    )
    partial_value = jnp.dot(
        gram_tile, residual_whole.astype(jnp.float32), precision=lax.Precision.HIGHEST
    )
    gram_prod = lax.psum(partial_value, "mp") / (cells_here * slab_count)
    data_update = (gram_prod + residual_cols.astype(jnp.float32)).astype(jnp.bfloat16)
    summed = lax.psum_scatter(
        lax.dot_general(
            smooth, data_update, (((0,), (0,)), ((), ())), preferred_element_type=jnp.float32
        ),
        "dp",
        scatter_dimension=0,
        tiled=True,
    )
    model_update = summed / math.sqrt(rows_here * block_count)
    return (data_update, model_update)


def solution(mesh):
    in_specs = (
        P(None, None, "mp"),
        P(None, None, "mp"),
        P("dp"),
        P("dp"),
        P("dp", None),
        P("dp", None),
    )
    out_specs = (P("dp", None), P(("mp", "dp"), None))
    return jax.shard_map(
        per_device, mesh=mesh, in_specs=in_specs, out_specs=out_specs, check_vma=False
    )
```

profile of v0, /device:TPU:1, one launch (start us, length us, event | category | flops | bytes accessed | tf_op | source)
XLA Modules:
  0.0 661.7 jit_solution(15564410182115889151)
XLA Ops:
  7.2 0.8 compare_select_fusion.1
  8.0 0.7 compare_select_fusion
  8.7 0.8 copy.8
  9.5 9.6 %gather_fusion = bf16[192,4,2048]{2,1,0:T(4,128)(2,1)} fusion(bf16[64,4,2048]{2,1,0:T(4,128)(2,1)S(1)} %copy-done, s32[1024]{0:T(1024)S(1)} %pad_clamp_fusion.1), kind=kCustom, calls=%fused_computation | custom fusion | bytes 6292224 | tf_op jit(solution)/shard_map/gather | solution.py:37
  19.1 9.7 %gather_fusion.1 = bf16[192,4,2048]{2,1,0:T(4,128)(2,1)} fusion(bf16[16,4,2048]{2,1,0:T(4,128)(2,1)S(1)} %copy-done.1, s32[1024]{0:T(1024)S(1)} %pad_clamp_fusion), kind=kCustom, calls=%fused_computation.1 | custom fusion | bytes 6292224 | tf_op jit(solution)/shard_map/gather | solution.py:38
  28.8 9.7 %multiply_reduce_fusion = f32[192,2048]{1,0:T(8,128)S(1)} fusion(bf16[192,4,2048]{2,1,0:T(4,128)(2,1)} %gather_fusion.1, bf16[192,4,2048]{2,1,0:T(4,128)(2,1)} %gather_fusion, f32[192,4]{1,0:T(8,128)S(1)} %copy.8), kind=kLoop, calls=%fused_computation.2 | loop fusion | flops 7471104 | bytes 7867392 | tf_op jit(solution)/shard_map/reduce_sum | solution.py:39
  38.5 1.2 convert_bitcast_fusion
  39.7 0.0 all-gather.5.cloned.1.call-start
  39.8 0.7 all-gather.5.cloned.1.call-update
  40.5 0.3 copy.9
  40.8 0.1 fusion.20
  40.9 4.0 collective-permute-start
  45.0 1.3 collective-permute-start.1
  46.3 0.3 collective-permute-done
  46.6 5.8 collective-permute-done.1
  52.5 1.3 fusion.4
  53.8 0.1 fusion.19
  53.9 3.8 collective-permute-start.2
  57.7 1.5 collective-permute-start.3
  59.2 0.1 collective-permute-done.2
  59.3 7.2 %collective-permute-done.3 = f32[192,1,128]{2,1,0:T(1,128)S(1)} collective-permute-done((f32[192,1,128]{2,1,0:T(1,128)S(1)}, f32[192,1,128]{2,1,0:T(1,128)S(1)}, u32[]{:S(2)}, u32[]{:S(2)}) %collective-permute-start.3) | collective-permute-done | bytes 98336 | tf_op jit(solution)/shard_map/ppermute | solution.py:19
  66.5 1.3 fusion.10
  67.8 128.4 %all-gather.3.cloned.1.call-done = bf16[3072,2048]{1,0:T(8,128)(2,1)} async-done(((bf16[192,2048]{1,0:T(8,128)(2,1)}), bf16[3072,2048]{1,0:T(8,128)(2,1)}) %all-gather.3.cloned.1.call-update) | async-done | bytes 12582928 | tf_op jit(solution)/shard_map/all_gather | solution.py:48
  196.3 10.3 %fusion.15 = f32[192,3072]{1,0:T(8,128)} fusion(bf16[3072,2048]{1,0:T(8,128)(2,1)} %all-gather.3.cloned.1.call-done, bf16[24,8,16,128]{3,2,1,0:T(8,128)(2,1)S(1)} %bitcast.15), kind=kOutput, calls=%fused_computation.28 | convolution fusion | flops 2415919104 | bytes 15728640 | tf_op jit(solution)/shard_map/dot_general | solution.py:46
  206.5 50.8 %all-gather.5.cloned.1.call-done = bf16[3072,256]{1,0:T(8,128)(2,1)} async-done(((bf16[192,256]{1,0:T(8,128)(2,1)}), bf16[3072,256]{1,0:T(8,128)(2,1)}) %all-gather.5.cloned.1.call-update) | async-done | bytes 1572880 | tf_op jit(solution)/shard_map/all_gather | solution.py:45
  257.3 4.0 fusion.21
  261.4 0.0 reduce-scatter.2.cloned.1.call-start
  261.4 272.9 %all-reduce.4.cloned.1.call-done = f32[192,256]{1,0:T(8,128)} async-done(((f32[192,256]{1,0:T(8,128)}), f32[192,256]{1,0:T(8,128)}) %all-reduce.4.cloned.1.call-update) | async-done | bytes 196624 | tf_op jit(solution)/shard_map/psum | solution.py:55
  534.3 1.0 add_convert_fusion
  535.2 1.8 fusion.13
  537.1 116.5 %reduce-scatter.2.cloned.1.call-done = f32[128,256]{1,0:T(8,128)} async-done(((f32[2048,256]{1,0:T(8,128)}), f32[128,256]{1,0:T(8,128)}) %reduce-scatter.2.cloned.1.call-update) | async-done | bytes 131088 | tf_op jit(solution)/shard_map/reduce_scatter | solution.py:57
  653.6 1.6 broadcast_multiply_fusion
  (15 shorter events, 0.2 us)
Async XLA Ops:
  7.2 2.3 copy-start
  7.2 189.1 %all-gather.3.cloned.1.call-start = ((), (), s32[]{:S(2)}) async-start(), calls=%async_computation.1 | async-start | bytes 13369344 | tf_op jit(solution)/shard_map/all_gather | solution.py:48
  9.5 9.6 %copy-start.1 = (bf16[16,4,2048]{2,1,0:T(4,128)(2,1)S(1)}, bf16[16,4,2048]{2,1,0:T(4,128)(2,1)}, u32[]{:S(2)}) copy-start(bf16[16,4,2048]{2,1,0:T(4,128)(2,1)} %param.6) | copy-start | bytes 786436
  39.7 217.6 %all-gather.5.cloned.1.call-start = ((), (), s32[]{:S(2)}) async-start(), calls=%async_computation.2 | async-start | bytes 1671168 | tf_op jit(solution)/shard_map/all_gather | solution.py:45
  40.5 493.8 %all-reduce.4.cloned.1.call-start = ((), (), s32[]{:S(2)}) async-start(), calls=%async_computation.3 | async-start | bytes 393216 | tf_op jit(solution)/shard_map/psum | solution.py:55
  40.9 5.7 collective-permute-start
  45.0 7.5 %collective-permute-start.1 = (f32[192,1,128]{2,1,0:T(1,128)S(1)}, f32[192,1,128]{2,1,0:T(1,128)S(1)}, u32[]{:S(2)}, u32[]{:S(2)}) collective-permute-start(f32[192,1,128]{2,1,0:T(1,128)S(1)} %get-tuple-element.7), channel_id=1, source_target_pairs={{16,0},{32,16},{48,32},{64,48},{80,64},{96,80},{112,96},{128,112},... | collective-permute-start | bytes 294920 | tf_op jit(solution)/shard_map/ppermute | solution.py:19
  53.9 5.4 collective-permute-start.2
  57.7 8.8 %collective-permute-start.3 = (f32[192,1,128]{2,1,0:T(1,128)S(1)}, f32[192,1,128]{2,1,0:T(1,128)S(1)}, u32[]{:S(2)}, u32[]{:S(2)}) collective-permute-start(f32[192,1,128]{2,1,0:T(1,128)S(1)} %get-tuple-element.5), channel_id=1, source_target_pairs={{16,0},{32,16},{48,32},{64,48},{80,64},{96,80},{112,96},{128,112},... | collective-permute-start | bytes 294920 | tf_op jit(solution)/shard_map/ppermute | solution.py:19
  206.5 327.7 %copy-start.3 = (bf16[192,256]{1,0:T(8,128)(2,1)S(1)}, bf16[192,256]{1,0:T(8,128)(2,1)}, u32[]{:S(2)}) copy-start(bf16[192,256]{1,0:T(8,128)(2,1)} %param.11) | copy-start | bytes 294916
  261.4 392.2 %reduce-scatter.2.cloned.1.call-start = ((), (), s32[]{:S(2)}) async-start(), calls=%async_computation.4 | async-start | bytes 2228224 | tf_op jit(solution)/shard_map/reduce_scatter | solution.py:57
  535.2 1.9 copy-start.2
Sparse Core Ops, SparseCore 0:
  39.8 156.4 all-gather.2
  199.5 57.7 all-gather.4
  261.5 272.7 all-reduce.3
  539.7 113.8 reduce-scatter.1
where the time goes:
time: 662 us
  waiting for transfers between devices  583 us (88%)
  local copies, waits for them, and re-layouts  20.7 us (3%)
  other arithmetic  17.5 us (3%)
  matrix products  16.1 us (2%)
  between operations  13.9 us (2%)
  starting transfers between devices  10.8 us (2%)
    psum x1, waiting for transfers between devices, per_device(): gram_prod = lax.psum(partial_value, 'mp') / (cells_here * slab_count)  273 us
    all_gather x1, waiting for transfers between devices, per_device(): lax.all_gather(sens, 'dp', axis=0, tiled=True)  128 us
    reduce_scatter x1, waiting for transfers between devices, per_device(): lax.psum_scatter(lax.dot_general(smooth, data_update, (((0,), (0,)), ((),...  116 us
    all_gather x1, waiting for transfers between devices, per_device(): residual_whole = lax.all_gather(residual_cols, 'dp', axis=0, tiled=True)  50.8 us
  transfers between devices with their start and end apart: 8, of which 8 were waited for; matrix products, arithmetic and copies ran while one was open for 2% of the time, Pallas kernels for 0%

commit v1 on v0

--- a/solution.py
+++ b/solution.py
@@ -6,6 +6,11 @@
 
 GRID_COLS = 128
 SWEEPS = 2
+
+
+def swapped_in(value, mesh_axis, dim):
+    outgoing = jnp.stack([value] * lax.axis_size(mesh_axis))
+    return jnp.concatenate(lax.all_to_all(outgoing, mesh_axis, 0, 0), axis=dim)
 
 
 def with_halo(array, sides, width):
@@ -45,7 +50,7 @@
     residual_whole = lax.all_gather(residual_cols, "dp", axis=0, tiled=True)
     gram_tile = lax.dot_general(
         smooth,
-        lax.all_gather(sens, "dp", axis=0, tiled=True),
+        swapped_in(sens, "dp", 0),
         (((1,), (1,)), ((), ())),
         preferred_element_type=jnp.float32,
     )

time: 662 us -> 793 us (1.20)
  waiting for transfers between devices: 583 us -> 699 us
  starting transfers between devices: 10.8 us -> 20.3 us
    ppermute x2, waiting for transfers between devices: 0.41 us -> 283 us  [with_halo(): before = lax.ppermute(last, axis, up)]
    all_gather x1 -> x0, waiting for transfers between devices: 128 us -> none  [per_device(): lax.all_gather(sens, 'dp', axis=0, tiled=True)]
    all_gather x1, waiting for transfers between devices: 50.8 us -> 0.01 us  [per_device(): residual_whole = lax.all_gather(residual_cols, 'dp', axis=0, tiled=True)]
    psum x1, waiting for transfers between devices: 273 us -> 294 us  [per_device(): gram_prod = lax.psum(partial_value, 'mp') / (cells_here * slab_count)]
    all_to_all x0 -> x1, starting transfers between devices: none -> 11.6 us  [swapped_in(): return jnp.concatenate(lax.all_to_all(outgoing, mesh_axis, 0, 0), axis=dim)]
    ppermute x2, waiting for transfers between devices: 13 us -> 3.95 us  [with_halo(): after = lax.ppermute(leading, axis, down)]
  transfers between devices with their start and end apart: 8 -> 8, of which waited for: 8 -> 6; matrix products, arithmetic and copies ran while one was open for 2% -> 2% of each run, Pallas kernels for 0% -> 0%
where the time goes in v1:
time: 793 us; the launch traced here: 792 us
  waiting for transfers between devices  699 us (88%)
  local copies, waits for them, and re-layouts  26.8 us (3%)
  starting transfers between devices  20.3 us (3%)
  other arithmetic  16.5 us (2%)
  matrix products  16.1 us (2%)
  between operations  13.9 us (2%)
    psum x1, waiting for transfers between devices, per_device(): gram_prod = lax.psum(partial_value, 'mp') / (cells_here * slab_count)  294 us
    ppermute x2, waiting for transfers between devices, with_halo(): before = lax.ppermute(last, axis, up)  283 us
    reduce_scatter x1, waiting for transfers between devices, per_device(): lax.psum_scatter(lax.dot_general(smooth, data_update, (((0,), (0,)), ((),...  117 us
  transfers between devices with their start and end apart: 8, of which 6 were waited for; matrix products, arithmetic and copies ran while one was open for 2% of the time, Pallas kernels for 0%

profile of v1, /device:TPU:1, one launch (start us, length us, event | category | flops | bytes accessed | tf_op | source)
XLA Modules:
  0.0 792.4 jit_solution(6061451918921055192)
XLA Ops:
  7.2 0.8 compare_select_fusion.1
  8.0 0.7 compare_select_fusion
  8.6 0.8 copy.8
  9.5 9.6 %gather_fusion = bf16[192,4,2048]{2,1,0:T(4,128)(2,1)} fusion(bf16[64,4,2048]{2,1,0:T(4,128)(2,1)S(1)} %copy-done, s32[1024]{0:T(1024)S(1)} %pad_clamp_fusion.1), kind=kCustom, calls=%fused_computation | custom fusion | bytes 6292224 | tf_op jit(solution)/shard_map/gather | solution.py:42
  19.1 9.7 %gather_fusion.1 = bf16[192,4,2048]{2,1,0:T(4,128)(2,1)} fusion(bf16[16,4,2048]{2,1,0:T(4,128)(2,1)S(1)} %copy-done.1, s32[1024]{0:T(1024)S(1)} %pad_clamp_fusion), kind=kCustom, calls=%fused_computation.1 | custom fusion | bytes 6292224 | tf_op jit(solution)/shard_map/gather | solution.py:43
  28.8 9.7 %multiply_reduce_fusion = f32[192,2048]{1,0:T(8,128)S(1)} fusion(bf16[192,4,2048]{2,1,0:T(4,128)(2,1)} %gather_fusion.1, bf16[192,4,2048]{2,1,0:T(4,128)(2,1)} %gather_fusion, f32[192,4]{1,0:T(8,128)S(1)} %copy.8), kind=kLoop, calls=%fused_computation.2 | loop fusion | flops 7471104 | bytes 7867392 | tf_op jit(solution)/shard_map/reduce_sum | solution.py:44
  38.4 0.2 convert_bitcast_fusion
  38.7 6.1 stack.2
  44.8 11.6 %all-to-all-start = ((bf16[16,192,2048]{2,1,0:T(8,128)(2,1)}), bf16[16,192,2048]{2,1,0:T(8,128)(2,1)}, u32[]{:S(2)}, u32[]{:S(2)}) async-start(bf16[16,192,2048]{2,1,0:T(8,128)(2,1)} %stack.2), calls=%async_computation | async-start | bytes 25165824 | tf_op jit(solution)/shard_map/all_to_all | solution.py:13
  56.4 0.7 all-gather.2.cloned.1.call-update
  57.0 0.0 all-reduce.4.cloned.1.call-start
  57.1 0.3 copy.9
  57.4 0.1 fusion.20
  57.5 1.8 collective-permute-start
  59.4 1.3 collective-permute-start.1
  60.7 283.3 %collective-permute-done = f32[192,1,128]{2,1,0:T(1,128)S(1)} collective-permute-done((f32[192,1,128]{2,1,0:T(1,128)S(1)}, f32[192,1,128]{2,1,0:T(1,128)S(1)}, u32[]{:S(2)}, u32[]{:S(2)}) %collective-permute-start) | collective-permute-done | bytes 98336 | tf_op jit(solution)/shard_map/ppermute | solution.py:23
  344.0 0.2 collective-permute-done.1
  344.2 1.3 fusion.4
  345.5 0.1 fusion.19
  345.7 4.0 collective-permute-start.2
  349.7 1.5 collective-permute-start.3
  351.2 0.1 collective-permute-done.2
  351.3 3.7 collective-permute-done.3
  355.0 1.3 fusion.10
  356.4 10.2 %fusion.15 = f32[192,3072]{1,0:T(8,128)} fusion(bf16[3072,2048]{1,0:T(8,128)(2,1)} %bitcast, bf16[24,8,16,128]{3,2,1,0:T(8,128)(2,1)S(1)} %bitcast.16), kind=kOutput, calls=%fused_computation.28 | convolution fusion | flops 2415919104 | bytes 15728640 | tf_op jit(solution)/shard_map/dot_general | solution.py:51
  366.6 4.0 fusion.21
  370.7 0.0 reduce-scatter.2.cloned.1.call-start
  370.7 294.1 %all-reduce.4.cloned.1.call-done = f32[192,256]{1,0:T(8,128)} async-done(((f32[192,256]{1,0:T(8,128)}), f32[192,256]{1,0:T(8,128)}) %all-reduce.4.cloned.1.call-update) | async-done | bytes 196624 | tf_op jit(solution)/shard_map/psum | solution.py:60
  664.9 1.0 add_convert_fusion
  665.8 1.8 fusion.13
  667.7 116.6 %reduce-scatter.2.cloned.1.call-done = f32[128,256]{1,0:T(8,128)} async-done(((f32[2048,256]{1,0:T(8,128)}), f32[128,256]{1,0:T(8,128)}) %reduce-scatter.2.cloned.1.call-update) | async-done | bytes 131088 | tf_op jit(solution)/shard_map/reduce_scatter | solution.py:62
  784.3 1.6 broadcast_multiply_fusion
  (15 shorter events, 0.1 us)
Async XLA Ops:
  7.2 2.3 copy-start
  9.5 9.6 %copy-start.1 = (bf16[16,4,2048]{2,1,0:T(4,128)(2,1)S(1)}, bf16[16,4,2048]{2,1,0:T(4,128)(2,1)}, u32[]{:S(2)}) copy-start(bf16[16,4,2048]{2,1,0:T(4,128)(2,1)} %param.6) | copy-start | bytes 786436
  44.8 311.6 %all-to-all-start = ((bf16[16,192,2048]{2,1,0:T(8,128)(2,1)}), bf16[16,192,2048]{2,1,0:T(8,128)(2,1)}, u32[]{:S(2)}, u32[]{:S(2)}) async-start(bf16[16,192,2048]{2,1,0:T(8,128)(2,1)} %stack.2), calls=%async_computation | async-start | bytes 25165824 | tf_op jit(solution)/shard_map/all_to_all | solution.py:13
  56.3 310.3 %all-gather.2.cloned.1.call-start = ((), (), s32[]{:S(2)}) async-start(), calls=%async_computation.2 | async-start | bytes 1671168 | tf_op jit(solution)/shard_map/all_gather | solution.py:50
  57.0 607.8 %all-reduce.4.cloned.1.call-start = ((), (), s32[]{:S(2)}) async-start(), calls=%async_computation.3 | async-start | bytes 393216 | tf_op jit(solution)/shard_map/psum | solution.py:60
  57.5 286.5 %collective-permute-start = (f32[192,1,128]{2,1,0:T(1,128)S(1)}, f32[192,1,128]{2,1,0:T(1,128)S(1)}, u32[]{:S(2)}, u32[]{:S(2)}) collective-permute-start(f32[192,1,128]{2,1,0:T(1,128)S(1)} %get-tuple-element.6), channel_id=1, source_target_pairs={{0,16},{16,32},{32,48},{48,64},{64,80},{80,96},{96,112},{112,128},... | collective-permute-start | bytes 294920 | tf_op jit(solution)/shard_map/ppermute | solution.py:23
  59.4 284.8 %collective-permute-start.1 = (f32[192,1,128]{2,1,0:T(1,128)S(1)}, f32[192,1,128]{2,1,0:T(1,128)S(1)}, u32[]{:S(2)}, u32[]{:S(2)}) collective-permute-start(f32[192,1,128]{2,1,0:T(1,128)S(1)} %get-tuple-element.7), channel_id=1, source_target_pairs={{16,0},{32,16},{48,32},{64,48},{80,64},{96,80},{112,96},{128,112},... | collective-permute-start | bytes 294920 | tf_op jit(solution)/shard_map/ppermute | solution.py:24
  345.7 5.6 collective-permute-start.2
  349.7 5.4 collective-permute-start.3
  366.6 298.3 %copy-start.3 = (bf16[192,256]{1,0:T(8,128)(2,1)S(1)}, bf16[192,256]{1,0:T(8,128)(2,1)}, u32[]{:S(2)}) copy-start(bf16[192,256]{1,0:T(8,128)(2,1)} %param.11) | copy-start | bytes 294916
  370.7 413.6 %reduce-scatter.2.cloned.1.call-start = ((), (), s32[]{:S(2)}) async-start(), calls=%async_computation.4 | async-start | bytes 2228224 | tf_op jit(solution)/shard_map/reduce_scatter | solution.py:62
  665.8 1.9 copy-start.2
Sparse Core Ops, SparseCore 0:
  60.4 127.3 all-gather.1
  370.8 294.0 all-reduce.3
  670.4 113.8 reduce-scatter.1
